TPU v7x, 32 devices: a whole 2x2x4 slice. The times are simulated.
32 devices in a mesh: groups: 2 (over y), gx: 4 (over z), gy: 4 (over x, core).
Axes of the slice: x: 2, y: 2, z: 4, core: 2. Of those that a mesh axis runs over, the one named last changes fastest.
Arguments:
- local_grad: float32 [49, 32, 16, 32], P(None, ('groups', 'gx'), 'gy'), parts along dimension 1, may hold values from -6 to 6
- translation: bfloat16 [7, 7, 7, 49, 49], replicated, may hold values from -0.0625 to 0.0625
- basis: bfloat16 [49, 131072], P(None, ('groups', 'gx', 'gy')), parts along dimension 1, may hold values from -0.875 to 0.875
- basis_grad: bfloat16 [3, 49, 131072], P(None, None, ('groups', 'gx', 'gy')), parts along dimension 2, may hold values from -0.875 to 0.875
- charges: float32 [131072], P(('groups', 'gx', 'gy')), parts along dimension 0, may hold values from -5 to 5
- atom_leaf: int32 [131072], P(('groups', 'gx', 'gy')), parts along dimension 0, may hold values from 0 to 8191, as said below
Outputs:
- leaf_mgrad: float32 [49, 32, 16, 32], P(None, ('groups', 'gx'), 'gy'), parts along dimension 1
- charge_grad: float32 [131072], P(('groups', 'gx', 'gy')), parts along dimension 0
- forces: float32 [3, 131072], P(None, ('groups', 'gx', 'gy')), parts along dimension 1
There are 2 independent parts, one for each index of `groups`. A program takes and returns all parts, laid end to end along the dimension named above; an argument that names none is the same for every part. Nothing has to cross between parts.
Inputs may be any that keep to these rules, and one draw needn't show every extreme that they name: atom_leaf[i] = (x * 16 + y) * 32 + z for the leaf box (x, y, z) of atom i; that box lies in the block of leaf boxes of the device that holds the atom or in a box next to that block.
All inputs are finite; a program needn't handle non-finite values.
Results may differ from a plain program's by a relative error of at most 0.0041.
Values may be sent and summed in bfloat16 or wider, within the bound.
A program may use at most 128 MiB of HBM per device.

v0:
```python
import jax
import jax.numpy as jnp
from jax import lax
from jax.sharding import PartitionSpec as P


def with_halo(block, sides, width):
    for axis, dim in sides:
        count = lax.axis_size(axis)
        forward = [(i, i + 1) for i in range(count - 1)]
        backward = [(target, source) for source, target in forward]
        low = lax.ppermute(
            lax.slice_in_dim(block, block.shape[dim] - width, None, axis=dim), axis, forward
        )
        high = lax.ppermute(lax.slice_in_dim(block, 0, width, axis=dim), axis, backward)
        block = jnp.concatenate([low, block, high], axis=dim)
    return block


def class_kernel(translation):
    extent = translation.shape[0]
    offset = jnp.abs(jnp.arange(extent) - 3)
    far_mask = (
        (offset[:, None, None] >= 2) | (offset[None, :, None] >= 2) | (offset[None, None, :] >= 2)
    )
    masked = translation * far_mask[:, :, :, None, None].astype(translation.dtype)
    pieces = []
    for parity_x in range(2):
        for parity_y in range(2):
            for parity_z in range(2):
                sliced = masked[
                    parity_x : parity_x + 6, parity_y : parity_y + 6, parity_z : parity_z + 6
                ]
                pieces.append(sliced[::-1, ::-1, ::-1])
    stacked = jnp.stack(pieces, axis=4)
    coeffs = translation.shape[3]
    return stacked.reshape(6, 6, 6, coeffs, 8 * coeffs)


def far_adjoint(padded, kernel):
    coeffs = padded.shape[0]
    source = padded[None, :, 1:, 1:, 1:]
    result = lax.conv_general_dilated(
        source,
        kernel,
        (2, 2, 2),
        "VALID",
        dimension_numbers=("NCDHW", "DHWIO", "NCDHW"),
        preferred_element_type=jnp.float32,
    )
    half_x, half_y, half_z = (result.shape[2], result.shape[3], result.shape[4])
    result = result.reshape(2, 2, 2, coeffs, half_x, half_y, half_z)
    result = jnp.transpose(result, (3, 4, 0, 5, 1, 6, 2))
    return result.reshape(coeffs, 2 * half_x, 2 * half_y, 2 * half_z)


def on_device(local_grad, translation, basis, basis_grad, charges, atom_leaf):
    rounded = local_grad.astype(jnp.bfloat16)
    widened = with_halo(rounded, (("gx", 1), ("gy", 2)), 2)
    padded = jnp.pad(widened, ((0, 0), (1, 1), (1, 1), (3, 3)))
    leaf_mgrad = far_adjoint(padded, class_kernel(translation))
    bordered = with_halo(leaf_mgrad.astype(jnp.bfloat16), (("gx", 1), ("gy", 2)), 1)
    coeffs, width_x, width_y, depth_z = local_grad.shape
    rows_y = width_y * lax.axis_size("gy")
    start_x = lax.axis_index("gx") * width_x
    start_y = lax.axis_index("gy") * width_y
    plane_size = rows_y * depth_z
    local_x = atom_leaf // plane_size - start_x + 1
    local_y = atom_leaf // depth_z % rows_y - start_y + 1
    local_z = atom_leaf % depth_z
    flat_index = (local_x * (width_y + 2) + local_y) * depth_z + local_z
    gathered = jnp.take(bordered.reshape(coeffs, -1), flat_index, axis=1).astype(jnp.float32)
    charge_grad = jnp.sum(basis.astype(jnp.float32) * gathered, axis=0)
    forces = -charges[None, :] * jnp.sum(basis_grad.astype(jnp.float32) * gathered[None], axis=1)
    return (leaf_mgrad, charge_grad, forces)


def solution(mesh):
    in_specs = (
        P(None, ("groups", "gx"), "gy", None),
        P(),
        P(None, ("groups", "gx", "gy")),
        P(None, None, ("groups", "gx", "gy")),
        P(("groups", "gx", "gy")),
        P(("groups", "gx", "gy")),
    )
    out_specs = (
        P(None, ("groups", "gx"), "gy", None),
        P(("groups", "gx", "gy")),
        P(None, ("groups", "gx", "gy")),
    )
    return jax.shard_map(
        on_device, mesh=mesh, in_specs=in_specs, out_specs=out_specs, check_vma=False
    )
```

profile of v0, /device:TPU:1, one launch (start us, length us, event | category | flops | bytes accessed | tf_op | source)
XLA Modules:
  0.0 159.5 jit_solution(2315595949794293268)
XLA Ops:
  2.3 4.0 %collective-permute-start = (bf16[49,2,4,32]{0,3,2,1:T(8,128)(2,1)}, bf16[49,2,4,32]{0,3,2,1:T(8,128)(2,1)S(1)}, u32[]{:S(2)}, u32[]{:S(2)}) collective-permute-start(bf16[49,2,4,32]{0,3,2,1:T(8,128)(2,1)} %get-tuple-element.19), channel_id=1, source_target_pairs={{0,4},{4,8},{8,12},{1,5},{5,9},{9,13},{2,6},{6,10},{10,14},{3,7},{... | collective-permute-start | bytes 75272 | tf_op jit(solution)/shard_map/ppermute | solution.py:12
  11.7 3.4 %broadcast_multiply_fusion = bf16[7,7,7,49,49]{4,3,2,1,0:T(8,128)(2,1)S(1)} fusion(bf16[7,7,7,49,49]{4,3,2,1,0:T(8,128)(2,1)} %param.7, bf16[7,7,7]{2,1,0:T(8,128)(2,1)S(1)} %or_convert_fusion), kind=kLoop, calls=%fused_computation.18 | loop fusion | flops 823543 | bytes 3294858 | tf_op jit(solution)/shard_map/mul | solution.py:26
  15.2 6.3 %fusion.54 = (bf16[6,6,6,49,49]{4,3,2,1,0:T(8,128)(2,1)S(1)}, bf16[6,6,6,49,49]{4,3,2,1,0:T(8,128)(2,1)S(1)}, bf16[6,6,6,49,49]{4,3,2,1,0:T(8,128)(2,1)S(1)}, bf...) fusion(bf16[7,7,7,49,49]{4,3,2,1,0:T(8,128)(2,1)S(1)} %broadcas, ...), kind=kLoop, calls=%fused_computation.107 | loop fusion | bytes 16595712 | tf_op jit(solution)/shard_map/slice | solution.py:31
  21.5 2.4 %bitcast_dynamic-update-slice_fusion.7 = bf16[6,6,6,49,8,49]{5,3,2,1,0,4:T(8,128)(2,1)S(1)} fusion(bf16[6,6,6,49,49]{4,3,2,1,0:T(8,128)(2,1)} %get-tuple-element.12), kind=kLoop, calls=%fused_computation.10 | loop fusion | bytes 4133808
  23.9 2.6 %bitcast_dynamic-update-slice_fusion.6 = bf16[6,6,6,49,8,49]{5,3,2,1,0,4:T(8,128)(2,1)S(1)} fusion(bf16[6,6,6,49,8,49]{5,3,2,1,0,4:T(8,128)(2,1)S(1)} %bitcast_dynamic-update-slice_fusion.7, bf16[6,6,6,49,49]{4,3,2,1,0:T(8,128)(2,1)} %get-tuple-element.11), kind=kLoop, calls=%fused_computation.9 | loop fusion | bytes 4133808
  26.5 2.6 %bitcast_dynamic-update-slice_fusion.5 = bf16[6,6,6,49,8,49]{5,3,2,1,0,4:T(8,128)(2,1)S(1)} fusion(bf16[6,6,6,49,8,49]{5,3,2,1,0,4:T(8,128)(2,1)S(1)} %bitcast_dynamic-update-slice_fusion.6, bf16[6,6,6,49,49]{4,3,2,1,0:T(8,128)(2,1)} %get-tuple-element.10), kind=kLoop, calls=%fused_computation.8 | loop fusion | bytes 4133808
  29.1 2.6 %bitcast_dynamic-update-slice_fusion.4 = bf16[6,6,6,49,8,49]{5,3,2,1,0,4:T(8,128)(2,1)S(1)} fusion(bf16[6,6,6,49,8,49]{5,3,2,1,0,4:T(8,128)(2,1)S(1)} %bitcast_dynamic-update-slice_fusion.5, bf16[6,6,6,49,49]{4,3,2,1,0:T(8,128)(2,1)} %get-tuple-element.9), kind=kLoop, calls=%fused_computation.7 | loop fusion | bytes 4133808
  34.8 29.3 %copy.21 = bf16[6,6,6,49,8,49]{5,4,3,2,1,0:T(8,128)(2,1)} copy(bf16[6,6,6,49,8,49]{5,3,2,1,0,4:T(8,128)(2,1)S(1)} %bitcast_dynamic-update-slice_fusion) | data formatting | bytes 16595712 | tf_op jit(solution)/shard_map/stack | solution.py:35
  64.1 32.1 %reshape.98 = bf16[6,6,6,49,392]{4,3,2,1,0:T(8,128)(2,1)} reshape(bf16[6,6,6,49,8,49]{5,4,3,2,1,0:T(8,128)(2,1)} %copy.21) | data formatting | bytes 16595712 | tf_op jit(solution)/shard_map/reshape | solution.py:37
  96.3 4.0 %collective-permute-start.2 = (bf16[49,8,2,32]{0,3,2,1:T(8,128)(2,1)S(1)}, bf16[49,8,2,32]{0,3,2,1:T(8,128)(2,1)S(1)}, u32[]{:S(2)}, u32[]{:S(2)}) collective-permute-start(bf16[49,8,2,32]{0,3,2,1:T(8,128)(2,1)S(1)} %get-tuple-element.13), channel_id=1, source_target_pairs={{0,1},{1,2},{2,3},{4,5},{5,6},{6,7},{8,9},{9,10},{10,11},{12,13},{... | collective-permute-start | bytes 150536 | tf_op jit(solution)/shard_map/ppermute | solution.py:12
  100.3 2.1 %collective-permute-start.3 = (bf16[49,8,2,32]{0,3,2,1:T(8,128)(2,1)S(1)}, bf16[49,8,2,32]{0,3,2,1:T(8,128)(2,1)S(1)}, u32[]{:S(2)}, u32[]{:S(2)}) collective-permute-start(bf16[49,8,2,32]{0,3,2,1:T(8,128)(2,1)S(1)} %get-tuple-element.14), channel_id=1, source_target_pairs={{1,0},{2,1},{3,2},{5,4},{6,5},{7,6},{9,8},{10,9},{11,10},{13,12},{... | collective-permute-start | bytes 150536 | tf_op jit(solution)/shard_map/ppermute | solution.py:15
  102.6 4.2 %collective-permute-done.3 = bf16[49,8,2,32]{0,3,2,1:T(8,128)(2,1)S(1)} collective-permute-done((bf16[49,8,2,32]{0,3,2,1:T(8,128)(2,1)S(1)}, bf16[49,8,2,32]{0,3,2,1:T(8,128)(2,1)S(1)}, u32[]{:S(2)}, u32[]{:S(2)}) %collective-permute-start.3) | collective-permute-done | bytes 50208 | tf_op jit(solution)/shard_map/ppermute | solution.py:15
  106.8 6.0 %fusion.36 = bf16[49,9,9,1,37]{0,4,2,1,3:T(8,128)(2,1)S(1)} fusion(bf16[49,8,2,32]{0,3,2,1:T(8,128)(2,1)S(1)} %collective-permute-done.3, pred[49,10,10,38]{0,3,2,1:T(8,128)(4,1)S(1)} %get-tuple-element.22, bf16[49,2,4,32]{0,3,2,1:T(8,128)(2,1)S(1)} %collective-permute-done.1, pred[49,10,10,38]{0,3,2,1:T(8,128)(4,1)S(1)} %copy-done.1, ...), kind=kLoop, calls=%fused_computation.64 | loop fusion | flops 5580414 | bytes 2181382 | tf_op jit(solution)/shard_map/broadcast_in_dim | solution.py:42
  114.0 7.0 %fusion.20 = f32[2,2,8,3,392]{4,2,3,1,0:T(8,128)S(1)} fusion(bf16[6,6,6,49,392]{4,3,2,1,0:T(8,128)(2,1)} %reshape.98, bf16[49,9,9,1,7,5]{0,4,5,2,1,3:T(8,128)(2,1)S(1)} %slice.92, bf16[49,9,9,1,8,6]{0,4,5,2,1,3:T(8,128)(2,1)S(1)} %copy.20, pred[8,3]{0,1:T(4,128)(4,1)S(1)} %copy-done.6), kind=kOutput, calls=%fused_computation.45 | convolution fusion | flops 798727424 | bytes 9107262 | tf_op jit(solution)/shard_map/conv_general_dilated | solution.py:43
  121.8 4.3 %collective-permute-start.4 = (bf16[49,1,4,32]{0,3,2,1:T(8,128)(2,1)S(1)}, bf16[49,1,4,32]{0,3,2,1:T(8,128)(2,1)S(1)}, u32[]{:S(2)}, u32[]{:S(2)}) collective-permute-start(bf16[49,1,4,32]{0,3,2,1:T(8,128)(2,1)S(1)} %get-tuple-element.17), channel_id=1, source_target_pairs={{0,4},{4,8},{8,12},{1,5},{5,9},{9,13},{2,6},{6,10},{10,14},{3,7},{... | collective-permute-start | bytes 37640 | tf_op jit(solution)/shard_map/ppermute | solution.py:12
  127.5 3.3 %collective-permute-done.5 = bf16[49,1,4,32]{0,3,2,1:T(8,128)(2,1)S(1)} collective-permute-done((bf16[49,1,4,32]{0,3,2,1:T(8,128)(2,1)S(1)}, bf16[49,1,4,32]{0,3,2,1:T(8,128)(2,1)S(1)}, u32[]{:S(2)}, u32[]{:S(2)}) %collective-permute-start.5) | collective-permute-done | bytes 12576 | tf_op jit(solution)/shard_map/ppermute | solution.py:15
  130.8 3.2 %collective-permute-start.6 = (bf16[49,6,1,32]{0,3,2,1:T(8,128)(2,1)S(1)}, bf16[49,6,1,32]{0,3,2,1:T(8,128)(2,1)S(1)}, u32[]{:S(2)}, u32[]{:S(2)}) collective-permute-start(bf16[49,6,1,32]{0,3,2,1:T(8,128)(2,1)S(1)} %get-tuple-element.15), channel_id=1, source_target_pairs={{0,1},{1,2},{2,3},{4,5},{5,6},{6,7},{8,9},{9,10},{10,11},{12,13},{... | collective-permute-start | bytes 56456 | tf_op jit(solution)/shard_map/ppermute | solution.py:12
  134.0 1.9 %collective-permute-start.7 = (bf16[49,6,1,32]{0,3,2,1:T(8,128)(2,1)S(1)}, bf16[49,6,1,32]{0,3,2,1:T(8,128)(2,1)S(1)}, u32[]{:S(2)}, u32[]{:S(2)}) collective-permute-start(bf16[49,6,1,32]{0,3,2,1:T(8,128)(2,1)S(1)} %get-tuple-element.16), channel_id=1, source_target_pairs={{1,0},{2,1},{3,2},{5,4},{6,5},{7,6},{9,8},{10,9},{11,10},{13,12},{... | collective-permute-start | bytes 56456 | tf_op jit(solution)/shard_map/ppermute | solution.py:15
  136.0 1.4 copy.25
  137.4 2.0 %collective-permute-done.7 = bf16[49,6,1,32]{0,3,2,1:T(8,128)(2,1)S(1)} collective-permute-done((bf16[49,6,1,32]{0,3,2,1:T(8,128)(2,1)S(1)}, bf16[49,6,1,32]{0,3,2,1:T(8,128)(2,1)S(1)}, u32[]{:S(2)}, u32[]{:S(2)}) %collective-permute-start.7) | collective-permute-done | bytes 18848 | tf_op jit(solution)/shard_map/ppermute | solution.py:15
  139.5 12.1 %gather_fusion = bf16[4096,49]{1,0:T(8,128)(2,1)S(1)} fusion(bf16[49,1152]{0,1:T(8,128)(2,1)S(1)} %bitcast.44, s32[4096]{0:T(1024)S(1)} %broadcast_clamp_fusion), kind=kCustom, calls=%fused_computation | custom fusion | bytes 819200 | tf_op jit(solution)/shard_map/jit(_take)/gather | solution.py:72
  152.4 1.6 copy.26
  154.0 2.9 %multiply_reduce_fusion.1 = f32[4096]{0:T(1024)} fusion(bf16[49,4096]{0,1:T(8,128)(2,1)} %copy.25, bf16[4096,49]{1,0:T(8,128)(2,1)S(1)} %gather_fusion, pred[4096]{0:T(1024)(128)(4,1)S(1)} %get-tuple-element.3), kind=kLoop, calls=%fused_computation.20 | loop fusion | flops 999424 | bytes 823296 | tf_op jit(solution)/shard_map/reduce_sum | solution.py:73
  156.9 2.0 %multiply_reduce_fusion = f32[3,4096]{1,0:T(4,128)S(1)} fusion(bf16[3,49,4096]{2,1,0:T(8,128)(2,1)} %param.9, f32[49,4096]{1,0:T(8,128)} %copy.26), kind=kLoop, calls=%fused_computation.17 | loop fusion | flops 1794048 | bytes 2056192 | tf_op jit(solution)/shard_map/reduce_sum | solution.py:74
  (56 shorter events, 15.0 us)
Async XLA Ops:
  2.3 94.0 %collective-permute-start = (bf16[49,2,4,32]{0,3,2,1:T(8,128)(2,1)}, bf16[49,2,4,32]{0,3,2,1:T(8,128)(2,1)S(1)}, u32[]{:S(2)}, u32[]{:S(2)}) collective-permute-start(bf16[49,2,4,32]{0,3,2,1:T(8,128)(2,1)} %get-tuple-element.19), channel_id=1, source_target_pairs={{0,4},{4,8},{8,12},{1,5},{5,9},{9,13},{2,6},{6,10},{10,14},{3,7},{... | collective-permute-start | bytes 75272 | tf_op jit(solution)/shard_map/ppermute | solution.py:12
  6.3 89.9 %collective-permute-start.1 = (bf16[49,2,4,32]{0,3,2,1:T(8,128)(2,1)}, bf16[49,2,4,32]{0,3,2,1:T(8,128)(2,1)S(1)}, u32[]{:S(2)}, u32[]{:S(2)}) collective-permute-start(bf16[49,2,4,32]{0,3,2,1:T(8,128)(2,1)} %get-tuple-element.20), channel_id=1, source_target_pairs={{4,0},{8,4},{12,8},{5,1},{9,5},{13,9},{6,2},{10,6},{14,10},{7,3},{... | collective-permute-start | bytes 75272 | tf_op jit(solution)/shard_map/ppermute | solution.py:15
  64.1 42.7 %copy-start = (pred[49,10,10,38]{0,3,2,1:T(8,128)(4,1)S(1)}, pred[49,10,10,38]{0,3,2,1:T(8,128)(4,1)}, u32[]{:S(2)}) copy-start(pred[49,10,10,38]{0,3,2,1:T(8,128)(4,1)} %get-tuple-element.23) | copy-start | bytes 558604
  64.1 42.7 %copy-start.1 = (pred[49,10,10,38]{0,3,2,1:T(8,128)(4,1)S(1)}, pred[49,10,10,38]{0,3,2,1:T(8,128)(4,1)}, u32[]{:S(2)}) copy-start(pred[49,10,10,38]{0,3,2,1:T(8,128)(4,1)} %get-tuple-element.24) | copy-start | bytes 558604
  96.3 6.3 %collective-permute-start.2 = (bf16[49,8,2,32]{0,3,2,1:T(8,128)(2,1)S(1)}, bf16[49,8,2,32]{0,3,2,1:T(8,128)(2,1)S(1)}, u32[]{:S(2)}, u32[]{:S(2)}) collective-permute-start(bf16[49,8,2,32]{0,3,2,1:T(8,128)(2,1)S(1)} %get-tuple-element.13), channel_id=1, source_target_pairs={{0,1},{1,2},{2,3},{4,5},{5,6},{6,7},{8,9},{9,10},{10,11},{12,13},{... | collective-permute-start | bytes 150536 | tf_op jit(solution)/shard_map/ppermute | solution.py:12
  100.3 6.5 %collective-permute-start.3 = (bf16[49,8,2,32]{0,3,2,1:T(8,128)(2,1)S(1)}, bf16[49,8,2,32]{0,3,2,1:T(8,128)(2,1)S(1)}, u32[]{:S(2)}, u32[]{:S(2)}) collective-permute-start(bf16[49,8,2,32]{0,3,2,1:T(8,128)(2,1)S(1)} %get-tuple-element.14), channel_id=1, source_target_pairs={{1,0},{2,1},{3,2},{5,4},{6,5},{7,6},{9,8},{10,9},{11,10},{13,12},{... | collective-permute-start | bytes 150536 | tf_op jit(solution)/shard_map/ppermute | solution.py:15
  113.1 0.9 copy-start.6
  113.9 13.5 %copy-start.4 = (s32[4096]{0:T(1024)S(1)}, s32[4096]{0:T(1024)}, u32[]{:S(2)}) copy-start(s32[4096]{0:T(1024)} %param.11) | copy-start | bytes 49156
  113.9 22.0 %copy-start.5 = (f32[4096]{0:T(1024)S(1)}, f32[4096]{0:T(1024)}, u32[]{:S(2)}) copy-start(f32[4096]{0:T(1024)} %param.10) | copy-start | bytes 49156
  114.0 22.0 %copy-start.3 = (bf16[49,4096]{1,0:T(8,128)(2,1)S(1)}, bf16[49,4096]{1,0:T(8,128)(2,1)}, u32[]{:S(2)}) copy-start(bf16[49,4096]{1,0:T(8,128)(2,1)} %param.8) | copy-start | bytes 1204228
  121.8 29.9 %copy-start.2 = (f32[49,2,2,2,2,16,2]{0,6,5,4,3,2,1:T(2,128)}, f32[49,2,2,2,2,16,2]{0,6,5,4,3,2,1:T(2,128)S(1)}, u32[]{:S(2)}) copy-start(f32[49,2,2,2,2,16,2]{0,6,5,4,3,2,1:T(2,128)S(1)} %copy.24) | copy-start | bytes 301060
  121.8 5.6 %collective-permute-start.4 = (bf16[49,1,4,32]{0,3,2,1:T(8,128)(2,1)S(1)}, bf16[49,1,4,32]{0,3,2,1:T(8,128)(2,1)S(1)}, u32[]{:S(2)}, u32[]{:S(2)}) collective-permute-start(bf16[49,1,4,32]{0,3,2,1:T(8,128)(2,1)S(1)} %get-tuple-element.17), channel_id=1, source_target_pairs={{0,4},{4,8},{8,12},{1,5},{5,9},{9,13},{2,6},{6,10},{10,14},{3,7},{... | collective-permute-start | bytes 37640 | tf_op jit(solution)/shard_map/ppermute | solution.py:12
  126.1 4.7 %collective-permute-start.5 = (bf16[49,1,4,32]{0,3,2,1:T(8,128)(2,1)S(1)}, bf16[49,1,4,32]{0,3,2,1:T(8,128)(2,1)S(1)}, u32[]{:S(2)}, u32[]{:S(2)}) collective-permute-start(bf16[49,1,4,32]{0,3,2,1:T(8,128)(2,1)S(1)} %get-tuple-element.18), channel_id=1, source_target_pairs={{4,0},{8,4},{12,8},{5,1},{9,5},{13,9},{6,2},{10,6},{14,10},{7,3},{... | collective-permute-start | bytes 37640 | tf_op jit(solution)/shard_map/ppermute | solution.py:15
  130.8 6.6 %collective-permute-start.6 = (bf16[49,6,1,32]{0,3,2,1:T(8,128)(2,1)S(1)}, bf16[49,6,1,32]{0,3,2,1:T(8,128)(2,1)S(1)}, u32[]{:S(2)}, u32[]{:S(2)}) collective-permute-start(bf16[49,6,1,32]{0,3,2,1:T(8,128)(2,1)S(1)} %get-tuple-element.15), channel_id=1, source_target_pairs={{0,1},{1,2},{2,3},{4,5},{5,6},{6,7},{8,9},{9,10},{10,11},{12,13},{... | collective-permute-start | bytes 56456 | tf_op jit(solution)/shard_map/ppermute | solution.py:12
  134.0 5.4 %collective-permute-start.7 = (bf16[49,6,1,32]{0,3,2,1:T(8,128)(2,1)S(1)}, bf16[49,6,1,32]{0,3,2,1:T(8,128)(2,1)S(1)}, u32[]{:S(2)}, u32[]{:S(2)}) collective-permute-start(bf16[49,6,1,32]{0,3,2,1:T(8,128)(2,1)S(1)} %get-tuple-element.16), channel_id=1, source_target_pairs={{1,0},{2,1},{3,2},{5,4},{6,5},{7,6},{9,8},{10,9},{11,10},{13,12},{... | collective-permute-start | bytes 56456 | tf_op jit(solution)/shard_map/ppermute | solution.py:15
where the time goes:
time: 161 us; the launch traced here: 160 us
  local copies, waits for them, and re-layouts  98.5 us (61%)
  starting transfers between devices  22.1 us (14%)
  other arithmetic  21.4 us (13%)
  waiting for transfers between devices  9.54 us (6%)
  matrix products  7.01 us (4%)
    reshape x1, local copies, waits for them, and re-layouts, class_kernel(): return stacked.reshape(6, 6, 6, coeffs, 8 * coeffs)  32.1 us
    another operation x2, local copies, waits for them, and re-layouts, class_kernel(): stacked = jnp.stack(pieces, axis=4)  30 us
    ppermute x4, starting transfers between devices, with_halo(): lax.ppermute(lax.slice_in_dim(block, block.shape[dim] - width, None, axis...  15.5 us
    unnamed x22, local copies, waits for them, and re-layouts  13.8 us
    gather x1, local copies, waits for them, and re-layouts, on_device(): jnp.take(bordered.reshape(coeffs, -1), flat_index, axis=1)  12.1 us
    ppermute x4, waiting for transfers between devices, with_halo(): lax.ppermute(lax.slice_in_dim(block, 0, width, axis=dim), axis, backward)  9.53 us
    conv_general_dilated x1, matrix products, far_adjoint(): lax.conv_general_dilated(source, kernel, (2, 2, 2), 'VALID', dimension_nu...  7.01 us
    ppermute x4, starting transfers between devices, with_halo(): lax.ppermute(lax.slice_in_dim(block, 0, width, axis=dim), axis, backward)  6.65 us
  transfers between devices with their start and end apart: 8, of which 3 were waited for; matrix products, arithmetic and copies ran while one was open for 57% of the time, Pallas kernels for 0%

commit v1 on v0

v1 whole, which is shorter than its diff:
```python
import jax
import jax.numpy as jnp
from jax import lax
from jax.experimental import pallas as pl
from jax.experimental.pallas import tpu as pltpu
from jax.sharding import PartitionSpec as P

MESH = pl.DeviceIdType.MESH
LANES = 128
HALF = 64
DIRS = ((-1, 0), (1, 0), (0, -1), (0, 1), (-1, -1), (-1, 1), (1, -1), (1, 1))


def source_span(step, width, depth):
    if step == 0:
        return depth, width
    return (depth, depth) if step < 0 else (width, depth)


def target_span(step, width, depth):
    if step == 0:
        return depth, width
    return (width + depth, depth) if step < 0 else (0, depth)


def kernel(
    count_x,
    count_y,
    grad_hbm,
    trans_hbm,
    basis_hbm,
    bgrad_hbm,
    charges_ref,
    leaf_ref,
    mgrad_hbm,
    charge_ref,
    forces_ref,
    grad,
    wide,
    trans,
    basis,
    bgrad,
    packed,
    windows,
    weights,
    mgrad_wide,
    mgrad,
    boxes,
    picked,
    place,
    load_sem,
    trans_sem,
    send_sem,
    recv_sem,
    send2_sem,
    recv2_sem,
    out_sem,
):
    width_x, width_y, depth_z, coeffs = grad.shape
    pairs = depth_z // 2
    extent = trans.shape[0]
    atoms = leaf_ref.shape[1]
    gx, gy = lax.axis_index("gx"), lax.axis_index("gy")

    grad_copy = pltpu.make_async_copy(grad_hbm, grad, load_sem.at[0])
    grad_copy.start()
    for dx in range(extent):
        pltpu.make_async_copy(trans_hbm.at[dx], trans.at[dx], trans_sem.at[dx]).start()
    basis_copy = pltpu.make_async_copy(basis_hbm, basis, load_sem.at[1])
    bgrad_copy = pltpu.make_async_copy(bgrad_hbm, bgrad, load_sem.at[2])
    basis_copy.start()
    bgrad_copy.start()

    def exists(sx, sy):
        ok = None
        for here, step, count in ((gx, sx, count_x), (gy, sy, count_y)):
            if step:
                test = (here + step >= 0) & (here + step < count)
                ok = test if ok is None else ok & test
        return ok

    barrier = pltpu.get_barrier_semaphore()
    for sx, sy in DIRS:
        @pl.when(exists(sx, sy))
        def _():
            pl.semaphore_signal(
                barrier, inc=1, device_id={"gx": gx + sx, "gy": gy + sy}, device_id_type=MESH
            )

    def spans(which, sx, sy, depth):
        (x0, nx), (y0, ny) = which(sx, width_x, depth), which(sy, width_y, depth)
        return pl.ds(x0, nx), pl.ds(y0, ny)

    def exchange1(k):
        sx, sy = DIRS[k]
        src = spans(source_span, sx, sy, 2)
        dst = spans(target_span, sx, sy, 2)
        return pltpu.make_async_remote_copy(
            src_ref=packed.at[src[0], src[1]],
            dst_ref=packed.at[dst[0], dst[1]],
            send_sem=send_sem.at[k],
            recv_sem=recv_sem.at[k],
            device_id={"gx": gx + sx, "gy": gy + sy},
            device_id_type=MESH,
        )

    def exchange2(k):
        sx, sy = DIRS[k]
        src = spans(source_span, sx, sy, 1)
        dst = spans(target_span, sx, sy, 1)
        return pltpu.make_async_remote_copy(
            src_ref=boxes.at[src[0], src[1]],
            dst_ref=boxes.at[dst[0], dst[1]],
            send_sem=send2_sem.at[k],
            recv_sem=recv2_sem.at[k],
            device_id={"gx": gx + sx, "gy": gy + sy},
            device_id_type=MESH,
        )

    wide[...] = jnp.zeros_like(wide)
    grad_copy.wait()
    wide[:, :, :, :coeffs] = grad[...]
    for x in range(width_x):
        for y in range(width_y):
            even = wide[x, y, pl.ds(0, pairs, stride=2), :]
            odd = wide[x, y, pl.ds(1, pairs, stride=2), :]
            both = odd + pltpu.roll(even, HALF, 1)
            packed[2 + x, 2 + y] = both.astype(jnp.bfloat16)

    def span_of(here, count):
        return jnp.minimum(here + 1, count - 1) - jnp.maximum(here - 1, 0) + 1

    pl.semaphore_wait(barrier, span_of(gx, count_x) * span_of(gy, count_y) - 1)

    for k, (sx, sy) in enumerate(DIRS):
        @pl.when(exists(sx, sy))
        def _():
            exchange1(k).start()

        @pl.when(jnp.logical_not(exists(sx, sy)))
        def _():
            x, y = spans(target_span, -sx, -sy, 2)
            packed[x, y] = jnp.zeros((x.size, y.size, pairs, LANES), jnp.bfloat16)
            x, y = spans(target_span, -sx, -sy, 1)
            boxes[x, y] = jnp.zeros((x.size, y.size, pairs, LANES), jnp.bfloat16)

    leaf = leaf_ref[...]
    rows_y = width_y * count_y
    plane = rows_y * depth_z
    lx = leaf // plane - gx * width_x
    ly = leaf // depth_z % rows_y - gy * width_y
    z = leaf % depth_z
    in_x = (lx >= 0) & (lx < width_x)
    in_y = (ly >= 0) & (ly < width_y)
    own_cols = width_x * width_y
    face_x = jnp.where(lx < 0, 0, width_y) + ly
    face_y = 2 * width_y + jnp.where(ly < 0, 0, width_x) + lx
    corner = 2 * (width_x + width_y) + jnp.where(lx < 0, 0, 2) + jnp.where(ly < 0, 0, 1)
    column = jnp.where(
        in_x & in_y,
        lx * width_y + ly,
        own_cols + jnp.where(in_y, face_x, jnp.where(in_x, face_y, corner)),
    )
    place[0:1, :] = column * pairs + z // 2
    place[1:2, :] = z % 2

    def prepare(dx, carry):
        pltpu.make_async_copy(trans_hbm.at[dx], trans.at[dx], trans_sem.at[dx]).wait()
        for dy in range(extent):
            blocks = []
            for dz in range(extent):
                one = trans[dx, dy, dz]
                blocks.append(jnp.pad(one, ((0, HALF - coeffs), (0, HALF - coeffs))))
            for m in range(extent - 1):
                weights[dx, dy, m * HALF : (m + 1) * HALF, :] = jnp.concatenate(
                    [blocks[m], blocks[m + 1]], axis=1
                )
        return carry

    lax.fori_loop(0, extent, prepare, 0)
    low_lanes = lax.broadcasted_iota(jnp.int32, (HALF, LANES), 1) < HALF
    for dx in range(2, extent - 2):
        for dy in range(2, extent - 2):
            first, last = pl.ds(HALF, HALF), pl.ds(4 * HALF, HALF)
            head = weights[dx, dy, first, :].astype(jnp.float32)
            weights[dx, dy, first, :] = jnp.where(low_lanes, head, 0.0).astype(jnp.bfloat16)
            weights[dx, dy, pl.ds(2 * HALF, 2 * HALF), :] = jnp.zeros(
                (2 * HALF, LANES), jnp.bfloat16
            )
            tail = weights[dx, dy, last, :].astype(jnp.float32)
            weights[dx, dy, last, :] = jnp.where(low_lanes, 0.0, tail).astype(jnp.bfloat16)

    for k, (sx, sy) in enumerate(DIRS):
        @pl.when(exists(-sx, -sy))
        def _():
            exchange1(k).wait_recv()

    row = lax.broadcasted_iota(jnp.int32, (pairs, LANES), 0)

    def window(x, carry):
        for y in range(width_y + 4):
            here = packed[x, y]
            value = here.astype(jnp.float32)
            after = jnp.where(row == pairs - 1, 0.0, pltpu.roll(value, pairs - 1, 0))
            before = jnp.where(row == 0, 0.0, pltpu.roll(value, 1, 0))
            windows[x, y, :, 0:LANES] = after.astype(jnp.bfloat16)
            windows[x, y, :, LANES : 2 * LANES] = here
            windows[x, y, :, 2 * LANES : 3 * LANES] = before.astype(jnp.bfloat16)
        return carry

    lax.fori_loop(0, width_x + 4, window, 0)

    halves_x, halves_y = width_x // 2, width_y // 2
    depth_k = (extent - 1) * HALF

    def step(i, totals):
        lhs = jnp.concatenate(
            [
                jnp.concatenate(
                    [
                        windows[2 * hx + 5 - i, 2 * hy + 5 - j]
                        for hx in range(halves_x)
                        for hy in range(halves_y)
                    ],
                    axis=0,
                )
                for j in range(extent - 1)
            ],
            axis=1,
        )
        out = []
        for py in range(2):
            rhs = jnp.concatenate(
                [
                    weights[i + px, py : py + extent - 1].reshape((extent - 1) * depth_k, LANES)
                    for px in range(2)
                ],
                axis=1,
            )
            out.append(totals[py] + jnp.dot(lhs, rhs, preferred_element_type=jnp.float32))
        return tuple(out)

    rows = halves_x * halves_y * pairs
    zero = jnp.zeros((rows, 2 * LANES), jnp.float32)
    totals = lax.fori_loop(0, extent - 1, step, (zero, zero))

    for py in range(2):
        for px in range(2):
            for hx in range(halves_x):
                for hy in range(halves_y):
                    start = (hx * halves_y + hy) * pairs
                    part = totals[py][start : start + pairs, px * LANES : (px + 1) * LANES]
                    x, y = 2 * hx + px, 2 * hy + py
                    boxes[1 + x, 1 + y] = part.astype(jnp.bfloat16)
                    mgrad_wide[x, y, pl.ds(0, pairs, stride=2), :] = part
                    mgrad_wide[x, y, pl.ds(1, pairs, stride=2), :] = pltpu.roll(part, HALF, 1)

    for k, (sx, sy) in enumerate(DIRS):
        @pl.when(exists(sx, sy))
        def _():
            exchange2(k).start()

    mgrad[...] = mgrad_wide[:, :, :, :coeffs]
    mgrad_copy = pltpu.make_async_copy(mgrad, mgrad_hbm, out_sem)
    mgrad_copy.start()

    chunk = 256
    own_rows = own_cols * pairs

    def turned(columns):
        return jnp.concatenate([boxes[x, y] for x, y in columns], axis=0).astype(jnp.float32).T.astype(
            jnp.bfloat16
        )

    def picks(base, size, at):
        local = (place[0:1, at] - base).astype(jnp.float32).astype(jnp.bfloat16)
        ids = lax.broadcasted_iota(jnp.int32, (size, chunk), 0).astype(jnp.bfloat16)
        return jnp.where(ids == local, jnp.bfloat16(1), jnp.bfloat16(0))

    def chosen(both, at):
        odd = place[1:2, at] == 1
        return jnp.where(odd, both[HALF:], both[:HALF])

    own = turned([(1 + x, 1 + y) for x in range(width_x) for y in range(width_y)])

    def pick_own(c, carry):
        at = pl.ds(pl.multiple_of(c * chunk, chunk), chunk)
        both = jnp.dot(own, picks(0, own_rows, at), preferred_element_type=jnp.float32)
        picked[:, at] = chosen(both, at)
        return carry

    lax.fori_loop(0, atoms // chunk, pick_own, 0)

    for k, (sx, sy) in enumerate(DIRS):
        @pl.when(exists(-sx, -sy))
        def _():
            exchange2(k).wait_recv()

    last_x, last_y = width_x + 1, width_y + 1
    ring = (
        [(0, 1 + y) for y in range(width_y)]
        + [(last_x, 1 + y) for y in range(width_y)]
        + [(1 + x, 0) for x in range(width_x)]
        + [(1 + x, last_y) for x in range(width_x)]
        + [(0, 0), (0, last_y), (last_x, 0), (last_x, last_y)]
    )
    outer = turned(ring)
    outer_rows = len(ring) * pairs
    basis_copy.wait()
    bgrad_copy.wait()

    def pick_outer(c, carry):
        at = pl.ds(pl.multiple_of(c * chunk, chunk), chunk)
        both = None
        for low in range(0, outer_rows, 256):
            size = min(256, outer_rows - low)
            term = jnp.dot(
                outer[:, low : low + size],
                picks(own_rows + low, size, at),
                preferred_element_type=jnp.float32,
            )
            both = term if both is None else both + term
        gathered = (picked[:, at] + chosen(both, at))[:coeffs]
        charge_ref[:, at] = jnp.sum(
            basis[:, at].astype(jnp.float32) * gathered, axis=0, keepdims=True
        )
        minus = -charges_ref[:, at]
        for a in range(3):
            forces_ref[a : a + 1, at] = minus * jnp.sum(
                bgrad[a, :, at].astype(jnp.float32) * gathered, axis=0, keepdims=True
            )
        return carry

    lax.fori_loop(0, atoms // chunk, pick_outer, 0)

    for k, (sx, sy) in enumerate(DIRS):
        @pl.when(exists(sx, sy))
        def _():
            exchange1(k).wait_send()
            exchange2(k).wait_send()
    mgrad_copy.wait()


def on_device(local_grad, translation, basis, basis_grad, charges, atom_leaf):
    coeffs, width_x, width_y, depth_z = local_grad.shape
    atoms = charges.shape[0]
    count_x, count_y = lax.axis_size("gx"), lax.axis_size("gy")
    extent = translation.shape[0]
    pairs = depth_z // 2
    grad = jnp.transpose(local_grad, (1, 2, 3, 0))
    block = (width_x, width_y, depth_z)
    f32, bf16 = jnp.float32, jnp.bfloat16

    def body(*refs):
        kernel(count_x, count_y, *refs)

    vmem = pl.BlockSpec(memory_space=pltpu.VMEM)
    hbm = pl.BlockSpec(memory_space=pl.ANY)
    dirs = len(DIRS)
    mgrad, charge_grad, forces = pl.pallas_call(
        body,
        out_shape=(
            jax.ShapeDtypeStruct(block + (coeffs,), f32),
            jax.ShapeDtypeStruct((1, atoms), f32),
            jax.ShapeDtypeStruct((3, atoms), f32),
        ),
        in_specs=[hbm, hbm, hbm, hbm, vmem, vmem],
        out_specs=(hbm, vmem, vmem),
        scratch_shapes=[
            pltpu.VMEM(block + (coeffs,), f32),
            pltpu.VMEM(block + (LANES,), f32),
            pltpu.VMEM(translation.shape, bf16),
            pltpu.VMEM(basis.shape, bf16),
            pltpu.VMEM(basis_grad.shape, bf16),
            pltpu.VMEM((width_x + 4, width_y + 4, pairs, LANES), bf16),
            pltpu.VMEM((width_x + 4, width_y + 4, pairs, 3 * LANES), bf16),
            pltpu.VMEM((extent, extent, (extent - 1) * HALF, LANES), bf16),
            pltpu.VMEM(block + (LANES,), f32),
            pltpu.VMEM(block + (coeffs,), f32),
            pltpu.VMEM((width_x + 2, width_y + 2, pairs, LANES), bf16),
            pltpu.VMEM((HALF, atoms), f32),
            pltpu.VMEM((8, atoms), jnp.int32),
            pltpu.SemaphoreType.DMA((3,)),
            pltpu.SemaphoreType.DMA((extent,)),
            pltpu.SemaphoreType.DMA((dirs,)),
            pltpu.SemaphoreType.DMA((dirs,)),
            pltpu.SemaphoreType.DMA((dirs,)),
            pltpu.SemaphoreType.DMA((dirs,)),
            pltpu.SemaphoreType.DMA,
        ],
        compiler_params=pltpu.CompilerParams(
            collective_id=0, has_side_effects=True, vmem_limit_bytes=48 * 2**20
        ),
        name="far_adjoint",
    )(grad, translation, basis, basis_grad, charges[None], atom_leaf[None])
    return (jnp.transpose(mgrad, (3, 0, 1, 2)), charge_grad[0], forces)


def solution(mesh):
    in_specs = (
        P(None, ("groups", "gx"), "gy", None),
        P(),
        P(None, ("groups", "gx", "gy")),
        P(None, None, ("groups", "gx", "gy")),
        P(("groups", "gx", "gy")),
        P(("groups", "gx", "gy")),
    )
    out_specs = (
        P(None, ("groups", "gx"), "gy", None),
        P(("groups", "gx", "gy")),
        P(None, ("groups", "gx", "gy")),
    )
    return jax.shard_map(
        on_device, mesh=mesh, in_specs=in_specs, out_specs=out_specs, check_vma=False
    )
```

time: 161 us -> 26.3 us (0.16)
  local copies, waits for them, and re-layouts: 98.5 us -> 6.67 us
  starting transfers between devices: 22.1 us -> 0 us
  other arithmetic: 21.4 us -> 0 us
  Pallas kernels: 0 us -> 18.7 us
  waiting for transfers between devices: 9.54 us -> 0 us
  matrix products: 7.01 us -> 0 us
    reshape x2 -> x0, local copies, waits for them, and re-layouts: 32.6 us -> none  [the longest x1 32.1 us: class_kernel(): return stacked.reshape(6, 6, 6, coeffs, 8 * coeffs)]
    another operation x2 -> x0, local copies, waits for them, and re-layouts: 30 us -> none  [class_kernel(): stacked = jnp.stack(pieces, axis=4)]
    ppermute x8 -> x0, starting transfers between devices: 22.1 us -> none  [the longest x4 15.5 us: with_halo(): lax.ppermute(lax.slice_in_dim(block, block.shape[dim] - width, None, axis...]
    pallas_call x0 -> x1, Pallas kernels: none -> 18.7 us  [on_device(): pl.pallas_call(body, out_shape=(jax.ShapeDtypeStruct(block + (coeffs,), f...]
    gather x1 -> x0, local copies, waits for them, and re-layouts: 12.1 us -> none  [on_device(): jnp.take(bordered.reshape(coeffs, -1), flat_index, axis=1)]
    ppermute x8 -> x0, waiting for transfers between devices: 9.54 us -> none  [the longest x4 9.53 us: with_halo(): lax.ppermute(lax.slice_in_dim(block, 0, width, axis=dim), axis, backward)]
    unnamed x22 -> x13, local copies, waits for them, and re-layouts: 13.8 us -> 6.67 us
    conv_general_dilated x1 -> x0, matrix products: 7.01 us -> none  [far_adjoint(): lax.conv_general_dilated(source, kernel, (2, 2, 2), 'VALID', dimension_nu...]
  transfers between devices with their start and end apart: 8 -> 0, of which waited for: 3 -> 0; matrix products, arithmetic and copies ran while one was open for 57% -> 0% of each run, Pallas kernels for 0% -> 0%
where the time goes in v1:
time: 26.3 us; the launch traced here: 26 us
  Pallas kernels  18.7 us (71%)
  local copies, waits for them, and re-layouts  6.67 us (25%)
  between operations  0.65 us (2%)
    pallas_call x1, Pallas kernels, on_device(): pl.pallas_call(body, out_shape=(jax.ShapeDtypeStruct(block + (coeffs,), f...  18.7 us
    unnamed x13, local copies, waits for them, and re-layouts  6.67 us

profile of v1, /device:TPU:1, one launch (start us, length us, event | category | flops | bytes accessed | tf_op | source)
XLA Modules:
  0.0 26.0 jit_solution(6893665428689252418)
XLA Ops:
  0.6 0.0 copy-start
  0.6 1.3 %copy-done = bf16[3,49,4096]{2,1,0:T(8,128)(2,1)S(1)} copy-done((bf16[3,49,4096]{2,1,0:T(8,128)(2,1)S(1)}, bf16[3,49,4096]{2,1,0:T(8,128)(2,1)}, u32[]{:S(2)}) %copy-start) | copy-done | bytes 1204248
  2.0 0.0 copy-start.1
  2.0 1.0 %copy-done.1 = bf16[49,4096]{1,0:T(8,128)(2,1)S(1)} copy-done((bf16[49,4096]{1,0:T(8,128)(2,1)S(1)}, bf16[49,4096]{1,0:T(8,128)(2,1)}, u32[]{:S(2)}) %copy-start.1) | copy-done | bytes 401432
  3.0 0.0 copy-start.2
  3.0 0.9 %copy-done.2 = f32[49,4,4,32]{0,3,2,1:T(8,128)S(1)} copy-done((f32[49,4,4,32]{0,3,2,1:T(8,128)S(1)}, f32[49,4,4,32]{0,3,2,1:T(8,128)}, u32[]{:S(2)}) %copy-start.2) | copy-done | bytes 100376
  3.9 0.0 copy-start.3
  3.9 0.7 %copy-done.3 = f32[4096]{0:T(1024)S(1)} copy-done((f32[4096]{0:T(1024)S(1)}, f32[4096]{0:T(1024)}, u32[]{:S(2)}) %copy-start.3) | copy-done | bytes 16408
  4.7 0.0 copy-start.4
  4.7 0.7 %copy-done.4 = s32[4096]{0:T(1024)S(1)} copy-done((s32[4096]{0:T(1024)S(1)}, s32[4096]{0:T(1024)}, u32[]{:S(2)}) %copy-start.4) | copy-done | bytes 16408
  5.4 18.7 %far_adjoint.1 = (f32[4,4,32,49]{3,2,1,0:T(8,128)S(1)}, f32[1,4096]{1,0:T(1,128)S(1)}, f32[3,4096]{1,0:T(4,128)S(1)}) custom-call(f32[4,4,32,49]{3,2,1,0:T(8,128)S(1)} %bitcast.6, bf16[7,7,7,49,49]{4,3,2,1,0:T(8,128)(2,1)} %refs_1_.1, bf16[49,4096]{1,0:T(8,128)(2,1)S(1)} %copy-done.1, bf16[3,49,4096]{2,1,0:T(8,128)(2,1)S(1)} %copy-done, ...), custom_call_target="tpu_custom_call" | custom-call | tf_op jit(solution)/shard_map/far_adjoint/pallas_call | solution.py:360
  24.1 0.7 %copy.12 = f32[49,4,4,32]{0,3,2,1:T(8,128)} copy(f32[49,4,4,32]{0,3,2,1:T(8,128)S(1)} %bitcast.5) | data formatting | bytes 200704
  24.8 0.6 %copy.13 = f32[4096]{0:T(1024)} copy(f32[4096]{0:T(1024)S(1)} %bitcast.9) | data formatting | bytes 32768
  25.4 0.6 %copy.14 = f32[3,4096]{1,0:T(4,128)} copy(f32[3,4096]{1,0:T(4,128)S(1)} %get-tuple-element.14) | data formatting | bytes 98304
Async XLA Ops:
  0.6 1.3 %copy-start = (bf16[3,49,4096]{2,1,0:T(8,128)(2,1)S(1)}, bf16[3,49,4096]{2,1,0:T(8,128)(2,1)}, u32[]{:S(2)}) copy-start(bf16[3,49,4096]{2,1,0:T(8,128)(2,1)} %refs_3_.1) | copy-start | bytes 3612676
  2.0 1.0 %copy-start.1 = (bf16[49,4096]{1,0:T(8,128)(2,1)S(1)}, bf16[49,4096]{1,0:T(8,128)(2,1)}, u32[]{:S(2)}) copy-start(bf16[49,4096]{1,0:T(8,128)(2,1)} %refs_2_.1) | copy-start | bytes 1204228
  3.0 0.9 %copy-start.2 = (f32[49,4,4,32]{0,3,2,1:T(8,128)S(1)}, f32[49,4,4,32]{0,3,2,1:T(8,128)}, u32[]{:S(2)}) copy-start(f32[49,4,4,32]{0,3,2,1:T(8,128)} %param.6) | copy-start | bytes 301060
  3.9 0.7 %copy-start.3 = (f32[4096]{0:T(1024)S(1)}, f32[4096]{0:T(1024)}, u32[]{:S(2)}) copy-start(f32[4096]{0:T(1024)} %param.10) | copy-start | bytes 49156
  4.7 0.7 %copy-start.4 = (s32[4096]{0:T(1024)S(1)}, s32[4096]{0:T(1024)}, u32[]{:S(2)}) copy-start(s32[4096]{0:T(1024)} %param.11) | copy-start | bytes 49156

commit v2 on v1

--- a/solution.py
+++ b/solution.py
@@ -8,6 +8,8 @@
 MESH = pl.DeviceIdType.MESH
 LANES = 128
 HALF = 64
+CHUNK = 256
+VMEM_LIMIT = 58 * 2**20
 DIRS = ((-1, 0), (1, 0), (0, -1), (0, 1), (-1, -1), (-1, 1), (1, -1), (1, 1))
 
 
@@ -21,6 +23,25 @@
     if step == 0:
         return depth, width
     return (width + depth, depth) if step < 0 else (0, depth)
+
+
+def split(value, size):
+    if size & (size - 1) == 0:
+        return value >> (size.bit_length() - 1), value & (size - 1)
+    quotient = lax.div(value, jnp.int32(size))
+    return quotient, value - quotient * size
+
+
+def picks(place, rows, base, size):
+    index = jnp.concatenate([place[pl.ds(r, 1), :] for r in rows], axis=1) >> 1
+    local = (index - base).astype(jnp.float32).astype(jnp.bfloat16)
+    ids = lax.broadcasted_iota(jnp.int32, (size, local.shape[1]), 0).astype(jnp.bfloat16)
+    return jnp.where(ids == local, jnp.bfloat16(1), jnp.bfloat16(0))
+
+
+def chosen(both, place, rows):
+    odd = jnp.concatenate([place[pl.ds(r, 1), :] for r in rows], axis=1) & 1
+    return jnp.where(odd == 1, both[HALF:], both[:HALF])
 
 
 def kernel(
@@ -28,48 +49,39 @@
     count_y,
     grad_hbm,
     trans_hbm,
-    basis_hbm,
-    bgrad_hbm,
-    charges_ref,
-    leaf_ref,
-    mgrad_hbm,
-    charge_ref,
-    forces_ref,
+    leaf_hbm,
+    mgrad,
+    outer,
+    picked,
+    place,
     grad,
     wide,
     trans,
-    basis,
-    bgrad,
+    leaf_in,
     packed,
     windows,
     weights,
     mgrad_wide,
-    mgrad,
     boxes,
-    picked,
-    place,
     load_sem,
     trans_sem,
     send_sem,
     recv_sem,
     send2_sem,
     recv2_sem,
-    out_sem,
 ):
     width_x, width_y, depth_z, coeffs = grad.shape
     pairs = depth_z // 2
     extent = trans.shape[0]
-    atoms = leaf_ref.shape[1]
+    atoms = picked.shape[1]
     gx, gy = lax.axis_index("gx"), lax.axis_index("gy")
 
     grad_copy = pltpu.make_async_copy(grad_hbm, grad, load_sem.at[0])
     grad_copy.start()
     for dx in range(extent):
         pltpu.make_async_copy(trans_hbm.at[dx], trans.at[dx], trans_sem.at[dx]).start()
-    basis_copy = pltpu.make_async_copy(basis_hbm, basis, load_sem.at[1])
-    bgrad_copy = pltpu.make_async_copy(bgrad_hbm, bgrad, load_sem.at[2])
-    basis_copy.start()
-    bgrad_copy.start()
+    leaf_copy = pltpu.make_async_copy(leaf_hbm, leaf_in, load_sem.at[1])
+    leaf_copy.start()
 
     def exists(sx, sy):
         ok = None
@@ -144,12 +156,11 @@
             x, y = spans(target_span, -sx, -sy, 1)
             boxes[x, y] = jnp.zeros((x.size, y.size, pairs, LANES), jnp.bfloat16)
 
-    leaf = leaf_ref[...]
-    rows_y = width_y * count_y
-    plane = rows_y * depth_z
-    lx = leaf // plane - gx * width_x
-    ly = leaf // depth_z % rows_y - gy * width_y
-    z = leaf % depth_z
+    leaf_copy.wait()
+    leaf = leaf_in[...]
+    rest, z = split(leaf, depth_z)
+    lx, ly = split(rest, width_y * count_y)
+    lx, ly = lx - gx * width_x, ly - gy * width_y
     in_x = (lx >= 0) & (lx < width_x)
     in_y = (ly >= 0) & (ly < width_y)
     own_cols = width_x * width_y
@@ -161,8 +172,7 @@
         lx * width_y + ly,
         own_cols + jnp.where(in_y, face_x, jnp.where(in_x, face_y, corner)),
     )
-    place[0:1, :] = column * pairs + z // 2
-    place[1:2, :] = z % 2
+    place[...] = column * depth_z + z
 
     def prepare(dx, carry):
         pltpu.make_async_copy(trans_hbm.at[dx], trans.at[dx], trans_sem.at[dx]).wait()
@@ -242,7 +252,7 @@
 
     rows = halves_x * halves_y * pairs
     zero = jnp.zeros((rows, 2 * LANES), jnp.float32)
-    totals = lax.fori_loop(0, extent - 1, step, (zero, zero))
+    totals = lax.fori_loop(0, extent - 1, step, (zero, zero), unroll=True)
 
     for py in range(2):
         for px in range(2):
@@ -261,10 +271,6 @@
             exchange2(k).start()
 
     mgrad[...] = mgrad_wide[:, :, :, :coeffs]
-    mgrad_copy = pltpu.make_async_copy(mgrad, mgrad_hbm, out_sem)
-    mgrad_copy.start()
-
-    chunk = 256
     own_rows = own_cols * pairs
 
     def turned(columns):
@@ -272,24 +278,18 @@
             jnp.bfloat16
         )
 
-    def picks(base, size, at):
-        local = (place[0:1, at] - base).astype(jnp.float32).astype(jnp.bfloat16)
-        ids = lax.broadcasted_iota(jnp.int32, (size, chunk), 0).astype(jnp.bfloat16)
-        return jnp.where(ids == local, jnp.bfloat16(1), jnp.bfloat16(0))
-
-    def chosen(both, at):
-        odd = place[1:2, at] == 1
-        return jnp.where(odd, both[HALF:], both[:HALF])
-
     own = turned([(1 + x, 1 + y) for x in range(width_x) for y in range(width_y)])
 
     def pick_own(c, carry):
-        at = pl.ds(pl.multiple_of(c * chunk, chunk), chunk)
-        both = jnp.dot(own, picks(0, own_rows, at), preferred_element_type=jnp.float32)
-        picked[:, at] = chosen(both, at)
+        at = pl.ds(pl.multiple_of(c * CHUNK, CHUNK), CHUNK)
+        rows = [c * (CHUNK // LANES) + r for r in range(CHUNK // LANES)]
+        both = jnp.dot(
+            own, picks(place, rows, 0, own_rows), preferred_element_type=jnp.float32
+        )
+        picked[:, at] = chosen(both, place, rows).astype(jnp.bfloat16)
         return carry
 
-    lax.fori_loop(0, atoms // chunk, pick_own, 0)
+    lax.fori_loop(0, atoms // CHUNK, pick_own, 0, unroll=4)
 
     for k, (sx, sy) in enumerate(DIRS):
         @pl.when(exists(-sx, -sy))
@@ -304,40 +304,73 @@
         + [(1 + x, last_y) for x in range(width_x)]
         + [(0, 0), (0, last_y), (last_x, 0), (last_x, last_y)]
     )
-    outer = turned(ring)
-    outer_rows = len(ring) * pairs
-    basis_copy.wait()
-    bgrad_copy.wait()
+    outer[...] = turned(ring)
+
+    for k, (sx, sy) in enumerate(DIRS):
+        @pl.when(exists(sx, sy))
+        def _():
+            exchange1(k).wait_send()
+            exchange2(k).wait_send()
+
+
+def tail(
+    own_rows,
+    mgrad_in,
+    outer_hbm,
+    picked_hbm,
+    place_hbm,
+    basis,
+    bgrad,
+    charges,
+    mgrad_hbm,
+    charge_ref,
+    forces_ref,
+    outer,
+    picked,
+    place,
+    mgrad,
+    load_sem,
+    out_sem,
+):
+    coeffs, atoms = basis.shape
+    loads = [
+        pltpu.make_async_copy(source, target, load_sem.at[k])
+        for k, (source, target) in enumerate(
+            ((mgrad_in, mgrad), (place_hbm, place), (outer_hbm, outer), (picked_hbm, picked))
+        )
+    ]
+    for load in loads:
+        load.start()
+    for load in loads:
+        load.wait()
+    mgrad_copy = pltpu.make_async_copy(mgrad, mgrad_hbm, out_sem)
+    mgrad_copy.start()
+    outer_rows = outer.shape[1]
 
     def pick_outer(c, carry):
-        at = pl.ds(pl.multiple_of(c * chunk, chunk), chunk)
+        at = pl.ds(pl.multiple_of(c * CHUNK, CHUNK), CHUNK)
+        rows = [c * (CHUNK // LANES) + r for r in range(CHUNK // LANES)]
         both = None
         for low in range(0, outer_rows, 256):
             size = min(256, outer_rows - low)
             term = jnp.dot(
                 outer[:, low : low + size],
-                picks(own_rows + low, size, at),
+                picks(place, rows, own_rows + low, size),
                 preferred_element_type=jnp.float32,
             )
             both = term if both is None else both + term
-        gathered = (picked[:, at] + chosen(both, at))[:coeffs]
+        gathered = (picked[:, at].astype(jnp.float32) + chosen(both, place, rows))[:coeffs]
         charge_ref[:, at] = jnp.sum(
             basis[:, at].astype(jnp.float32) * gathered, axis=0, keepdims=True
         )
-        minus = -charges_ref[:, at]
+        minus = -charges[:, at]
         for a in range(3):
             forces_ref[a : a + 1, at] = minus * jnp.sum(
                 bgrad[a, :, at].astype(jnp.float32) * gathered, axis=0, keepdims=True
             )
         return carry
 
-    lax.fori_loop(0, atoms // chunk, pick_outer, 0)
-
-    for k, (sx, sy) in enumerate(DIRS):
-        @pl.when(exists(sx, sy))
-        def _():
-            exchange1(k).wait_send()
-            exchange2(k).wait_send()
+    lax.fori_loop(0, atoms // CHUNK, pick_outer, 0, unroll=4)
     mgrad_copy.wait()
 
 
@@ -347,6 +380,7 @@
     count_x, count_y = lax.axis_size("gx"), lax.axis_size("gy")
     extent = translation.shape[0]
     pairs = depth_z // 2
+    outer_rows = (2 * (width_x + width_y) + 4) * pairs
     grad = jnp.transpose(local_grad, (1, 2, 3, 0))
     block = (width_x, width_y, depth_z)
     f32, bf16 = jnp.float32, jnp.bfloat16
@@ -354,45 +388,64 @@
     def body(*refs):
         kernel(count_x, count_y, *refs)
 
+    def tail_body(*refs):
+        tail(width_x * width_y * pairs, *refs)
+
     vmem = pl.BlockSpec(memory_space=pltpu.VMEM)
-    hbm = pl.BlockSpec(memory_space=pl.ANY)
+    hbm = pl.BlockSpec(memory_space=pltpu.HBM)
     dirs = len(DIRS)
+    mgrad, outer, picked, place = pl.pallas_call(
+        body,
+        out_shape=(
+            jax.ShapeDtypeStruct(block + (coeffs,), f32),
+            jax.ShapeDtypeStruct((LANES, outer_rows), bf16),
+            jax.ShapeDtypeStruct((HALF, atoms), bf16),
+            jax.ShapeDtypeStruct((atoms // LANES, LANES), jnp.int32),
+        ),
+        in_specs=[hbm, hbm, hbm],
+        out_specs=(vmem, vmem, vmem, vmem),
+        scratch_shapes=[
+            pltpu.VMEM(block + (coeffs,), f32),
+            pltpu.VMEM(block + (LANES,), f32),
+            pltpu.VMEM(translation.shape, bf16),
+            pltpu.VMEM((atoms // LANES, LANES), jnp.int32),
+            pltpu.VMEM((width_x + 4, width_y + 4, pairs, LANES), bf16),
+            pltpu.VMEM((width_x + 4, width_y + 4, pairs, 3 * LANES), bf16),
+            pltpu.VMEM((extent, extent, (extent - 1) * HALF, LANES), bf16),
+            pltpu.VMEM(block + (LANES,), f32),
+            pltpu.VMEM((width_x + 2, width_y + 2, pairs, LANES), bf16),
+            pltpu.SemaphoreType.DMA((2,)),
+            pltpu.SemaphoreType.DMA((extent,)),
+            pltpu.SemaphoreType.DMA((dirs,)),
+            pltpu.SemaphoreType.DMA((dirs,)),
+            pltpu.SemaphoreType.DMA((dirs,)),
+            pltpu.SemaphoreType.DMA((dirs,)),
+        ],
+        compiler_params=pltpu.CompilerParams(
+            collective_id=0, has_side_effects=True, vmem_limit_bytes=VMEM_LIMIT
+        ),
+        name="far_adjoint",
+    )(grad, translation, atom_leaf.reshape(atoms // LANES, LANES))
     mgrad, charge_grad, forces = pl.pallas_call(
-        body,
+        tail_body,
         out_shape=(
             jax.ShapeDtypeStruct(block + (coeffs,), f32),
             jax.ShapeDtypeStruct((1, atoms), f32),
             jax.ShapeDtypeStruct((3, atoms), f32),
         ),
-        in_specs=[hbm, hbm, hbm, hbm, vmem, vmem],
+        in_specs=[hbm] * 4 + [vmem] * 3,
         out_specs=(hbm, vmem, vmem),
         scratch_shapes=[
+            pltpu.VMEM((LANES, outer_rows), bf16),
+            pltpu.VMEM((HALF, atoms), bf16),
+            pltpu.VMEM((atoms // LANES, LANES), jnp.int32),
             pltpu.VMEM(block + (coeffs,), f32),
-            pltpu.VMEM(block + (LANES,), f32),
-            pltpu.VMEM(translation.shape, bf16),
-            pltpu.VMEM(basis.shape, bf16),
-            pltpu.VMEM(basis_grad.shape, bf16),
-            pltpu.VMEM((width_x + 4, width_y + 4, pairs, LANES), bf16),
-            pltpu.VMEM((width_x + 4, width_y + 4, pairs, 3 * LANES), bf16),
-            pltpu.VMEM((extent, extent, (extent - 1) * HALF, LANES), bf16),
-            pltpu.VMEM(block + (LANES,), f32),
-            pltpu.VMEM(block + (coeffs,), f32),
-            pltpu.VMEM((width_x + 2, width_y + 2, pairs, LANES), bf16),
-            pltpu.VMEM((HALF, atoms), f32),
-            pltpu.VMEM((8, atoms), jnp.int32),
-            pltpu.SemaphoreType.DMA((3,)),
-            pltpu.SemaphoreType.DMA((extent,)),
-            pltpu.SemaphoreType.DMA((dirs,)),
-            pltpu.SemaphoreType.DMA((dirs,)),
-            pltpu.SemaphoreType.DMA((dirs,)),
-            pltpu.SemaphoreType.DMA((dirs,)),
+            pltpu.SemaphoreType.DMA((4,)),
             pltpu.SemaphoreType.DMA,
         ],
-        compiler_params=pltpu.CompilerParams(
-            collective_id=0, has_side_effects=True, vmem_limit_bytes=48 * 2**20
-        ),
-        name="far_adjoint",
-    )(grad, translation, basis, basis_grad, charges[None], atom_leaf[None])
+        compiler_params=pltpu.CompilerParams(vmem_limit_bytes=VMEM_LIMIT),
+        name="atom_sums",
+    )(mgrad, outer, picked, place, basis, basis_grad, charges[None])
     return (jnp.transpose(mgrad, (3, 0, 1, 2)), charge_grad[0], forces)
 
 

time: 26.3 us -> 21.2 us (0.81)
  local copies, waits for them, and re-layouts: 6.67 us -> 0 us
  Pallas kernels: 18.7 us -> 20.4 us
    unnamed x13 -> x0, local copies, waits for them, and re-layouts: 6.67 us -> none
    pallas_call x0 -> x1, Pallas kernels: none -> 4.78 us  [on_device(): pl.pallas_call(tail_body, out_shape=(jax.ShapeDtypeStruct(block + (coeffs...]
    pallas_call x1, Pallas kernels: 18.7 us -> 15.6 us  [on_device(): pl.pallas_call(body, out_shape=(jax.ShapeDtypeStruct(block + (coeffs,), f...]
where the time goes in v2:
time: 21.2 us; the launch traced here: 21.1 us
  Pallas kernels  20.4 us (96%)
  between operations  0.64 us (3%)
    pallas_call x1, Pallas kernels, on_device(): pl.pallas_call(body, out_shape=(jax.ShapeDtypeStruct(block + (coeffs,), f...  15.6 us
    pallas_call x1, Pallas kernels, on_device(): pl.pallas_call(tail_body, out_shape=(jax.ShapeDtypeStruct(block + (coeffs...  4.78 us

profile of v2, /device:TPU:1, one launch (start us, length us, event | category | flops | bytes accessed | tf_op | source)
XLA Modules:
  0.0 21.1 jit_solution(3328026298615343961)
XLA Ops:
  0.6 15.6 %far_adjoint.1 = (f32[4,4,32,49]{3,2,1,0:T(8,128)}, bf16[128,320]{1,0:T(8,128)(2,1)}, bf16[64,4096]{1,0:T(8,128)(2,1)}, s32[32,128]{1,0:T(8,128)}) custom-call(f32[4,4,32,49]{3,2,1,0:T(8,128)} %bitcast.5, bf16[7,7,7,49,49]{4,3,2,1,0:T(8,128)(2,1)} %refs_1_.1, s32[32,128]{1,0:T(8,128)} %bitcast.6), custom_call_target="tpu_custom_call" | custom-call | tf_op jit(solution)/shard_map/far_adjoint/pallas_call | solution.py:397
  16.3 4.8 %atom_sums.1 = (f32[4,4,32,49]{3,2,1,0:T(8,128)}, f32[1,4096]{1,0:T(1,128)}, f32[3,4096]{1,0:T(4,128)}) custom-call(f32[4,4,32,49]{3,2,1,0:T(8,128)} %get-tuple-element.10.refs_0_, bf16[128,320]{1,0:T(8,128)(2,1)} %get-tuple-element.11.refs_1_, bf16[64,4096]{1,0:T(8,128)(2,1)} %get-tuple-element.12.refs_2_, s32[32,128]{1,0:T(8,128)} %get-tuple-element.13.refs_3_, ...), custom_call_target="tpu_custom_call" | custom-call | tf_op jit(solution)/shard_map/atom_sums/pallas_call | solution.py:429
